TPU v7x, 256 devices: a whole 4x4x8 slice. The times are simulated.
256 devices in a mesh: dp: 32 (over y, x, core), mp: 8 (over z).
Axes of the slice: x: 4, y: 4, z: 8, core: 2. Of those that a mesh axis runs over, the one named last changes fastest.
Arguments:
- patches: bfloat16 [4096, 588], P('dp'), may hold values from -6 to 6
- embed_weight: bfloat16 [6144, 588], P(('mp', 'dp')), may hold values from -0.25 to 0.25
- project_weight: bfloat16 [6144, 3, 3072], P('dp', None, 'mp'), may hold values from -0.078125 to 0.078125
- patch_counts: int32 [256], P('dp'), may hold values from 0 to 64, as said below
- segment_ids: int32 [4096], P('dp'), may hold values from -1 to 255, as said below
- targets: bfloat16 [4096, 3072], P('dp', 'mp'), may hold values from -4 to 4
Outputs:
- project_grad: float32 [6144, 3, 3072], P('dp', None, 'mp')
- loss_value: float32 [], replicated
Inputs may be any that keep to these rules, and one draw needn't show every extreme that they name: `patch_counts`: entry 8 * i + j is the number of patches of image slot j of device i along dp, a multiple of 16, 0 for an empty slot; the counts of one device add up to at most 128, and some device reaches it. `segment_ids`: the rows of device i along dp hold its images whole, slot after slot, each row carrying the id 8 * i + slot of its image, then -1 on the rows left. A device in the upper half of dp holds more rows than the device half the axis away. On each device the images that end after its row 96 cover at most 64 rows. Those rows plus all the rows of the device half the axis away come to at most 96. Both bounds are reached.
All inputs are finite; a program needn't handle non-finite values.
Results may differ from a plain program's by a relative error of at most 0.012.
The roundings to bfloat16 on the way count: a program that leaves them out, or rounds other values in their place, can miss the bound.
Values may be sent and summed in bfloat16 or wider, within the bound.
No kernel may reach another device: no remote copies, remote signals or barrier semaphores. Data moves between devices by JAX's collectives and lax.ppermute only.
A program may use at most 64 MiB of HBM per device.

v0:
```python
import math

import jax
import jax.numpy as jnp
from jax import lax
from jax.sharding import PartitionSpec as P

HD = 128


def layer_norm(values):
    center = values - jnp.mean(values, axis=-1, keepdims=True)
    spread = jnp.mean(center * center, axis=-1, keepdims=True)
    return center * lax.rsqrt(spread + 1e-06)


def norm_grad(values, cotangent):
    return jax.vjp(layer_norm, values)[1](cotangent)[0]


def attend_block(query_raw, key_raw, value_rows, segment, target):
    inverse_root = 1.0 / math.sqrt(HD)
    query_normed = layer_norm(query_raw).astype(jnp.bfloat16)
    key_normed = layer_norm(key_raw).astype(jnp.bfloat16)
    scores = (
        jnp.einsum("qhd,khd->hqk", query_normed, key_normed, preferred_element_type=jnp.float32)
        * inverse_root
    )
    valid = segment >= 0
    allowed = (segment[:, None] == segment[None, :]) & valid[:, None]
    exponent = jnp.where(allowed[None], jnp.exp(scores), 0.0)
    denominator = jnp.sum(exponent, axis=-1, keepdims=True)
    denominator = jnp.where(valid[None, :, None], denominator, 1.0)
    weights = (exponent / denominator).astype(jnp.bfloat16)
    attended = jnp.einsum("hqk,khd->qhd", weights, value_rows, preferred_element_type=jnp.float32)
    feature_count = attended.shape[1] * attended.shape[2]
    error_rows = jnp.where(
        valid[:, None], attended.reshape(-1, feature_count) - target.astype(jnp.float32), 0.0
    )
    squared_sum = jnp.sum(error_rows * error_rows)
    return (query_normed, key_normed, weights, error_rows, squared_sum)


def attend_back(
    query_raw, key_raw, query_normed, key_normed, value_rows, weights, error_rows, patch_total
):
    inverse_root = 1.0 / math.sqrt(HD)
    out_grad = (error_rows / patch_total).astype(jnp.bfloat16).reshape(query_normed.shape)
    prob_grad = jnp.einsum("qhd,khd->hqk", out_grad, value_rows, preferred_element_type=jnp.float32)
    value_grad = jnp.einsum(
        "hqk,qhd->khd", weights, out_grad, preferred_element_type=jnp.float32
    ).astype(jnp.bfloat16)
    weight_float = weights.astype(jnp.float32)
    score_grad = (
        weight_float
        * (prob_grad - jnp.sum(prob_grad * weight_float, axis=-1, keepdims=True))
        * inverse_root
    ).astype(jnp.bfloat16)
    normed_grad_q = jnp.einsum(
        "hqk,khd->qhd", score_grad, key_normed, preferred_element_type=jnp.float32
    )
    normed_grad_k = jnp.einsum(
        "hqk,qhd->khd", score_grad, query_normed, preferred_element_type=jnp.float32
    )
    query_grad = norm_grad(query_raw, normed_grad_q).astype(jnp.bfloat16)
    key_grad = norm_grad(key_raw, normed_grad_k).astype(jnp.bfloat16)
    return jnp.stack([query_grad, key_grad, value_grad], axis=1)


def local(patches, embed_weight, project_weight, patch_counts, segment_ids, targets):
    local_total = jnp.sum(patch_counts).astype(jnp.float32)
    row_total = patches.shape[0]
    own_features = jnp.einsum(
        "rp,cp->rc",
        patches,
        lax.all_gather(embed_weight, "dp", axis=0, tiled=True),
        preferred_element_type=jnp.float32,
    ).astype(jnp.bfloat16)
    embedded = lax.all_gather(own_features, "mp", axis=1, tiled=True)
    normed = layer_norm(embedded.astype(jnp.float32)).astype(jnp.bfloat16)
    flat_weight = project_weight.reshape(project_weight.shape[0], -1)
    section = normed
    projected = jnp.dot(
        section,
        lax.all_gather(flat_weight, "dp", axis=0, tiled=True),
        preferred_element_type=jnp.float32,
    )
    head_dev = project_weight.shape[2] // HD
    projected = projected.reshape(row_total, 3, head_dev, HD)
    query_raw = projected[:, 0]
    key_raw = projected[:, 1]
    value_rows = projected[:, 2].astype(jnp.bfloat16)
    query_normed, key_normed, weights, error_rows, squared_sum = attend_block(
        query_raw, key_raw, value_rows, segment_ids, targets
    )
    lead_flag = (lax.axis_index("mp") == 0).astype(jnp.float32)
    squared_all, patch_total = lax.psum((squared_sum, local_total * lead_flag), ("dp", "mp"))
    loss_value = squared_all / (2.0 * patch_total)
    grad_rows = attend_back(
        query_raw, key_raw, query_normed, key_normed, value_rows, weights, error_rows, patch_total
    )
    grad_rows = grad_rows.reshape(row_total, -1)
    normed_blocks = lax.all_to_all(normed, "dp", split_axis=1, concat_axis=0, tiled=True)
    section = normed_blocks
    weight_grad = lax.dot_general(
        section,
        lax.all_gather(grad_rows, "dp", axis=0, tiled=True),
        (((0,), (0,)), ((), ())),
        preferred_element_type=jnp.float32,
    )
    return (weight_grad.reshape(weight_grad.shape[0], 3, -1), loss_value)


def solution(mesh):
    in_specs = (
        P("dp", None),
        P(("mp", "dp"), None),
        P("dp", None, "mp"),
        P("dp"),
        P("dp"),
        P("dp", "mp"),
    )
    out_specs = (P("dp", None, "mp"), P())
    return jax.shard_map(local, mesh=mesh, in_specs=in_specs, out_specs=out_specs, check_vma=False)
```

profile of v0, /device:TPU:1, one launch (start us, length us, event | category | flops | bytes accessed | tf_op | source)
XLA Modules:
  0.0 326.8 jit_solution(9809502696654558383)
XLA Ops:
  7.3 26.7 %all_gather.12 = bf16[768,588]{1,0:T(8,128)(2,1)S(1)} all-gather(bf16[24,588]{1,0:T(8,128)(2,1)} %param.7), channel_id=1, replica_groups=mesh['dp'=32,'mp'=8] {'dp'}, dimensions={0}, use_global_device_ids=true | all-gather | bytes 931392 | tf_op jit(solution)/shard_map/all_gather | solution.py:76
  34.0 1.1 convolution_convert_fusion
  35.2 1.8 copy.44
  37.2 0.6 reduce_sum.134
  38.6 33.1 %all-gather.4.cloned.1.call-done = bf16[128,6144]{1,0:T(8,128)(2,1)} async-done(((bf16[128,768]{1,0:T(8,128)(2,1)}), bf16[128,6144]{1,0:T(8,128)(2,1)}) %all-gather.4.cloned.1.call-update) | async-done | bytes 1572880 | tf_op jit(solution)/shard_map/all_gather | solution.py:79
  71.8 1.8 convert_reduce_fusion
  73.6 2.0 fusion.3
  75.6 0.5 fusion.4
  76.1 73.2 %all-gather.6.cloned.1.call-done = bf16[6144,1152]{1,0:T(8,128)(2,1)} async-done(((bf16[192,1152]{1,0:T(8,128)(2,1)}), bf16[6144,1152]{1,0:T(8,128)(2,1)}) %all-gather.6.cloned.1.call-update) | async-done | bytes 14155792 | tf_op jit(solution)/shard_map/all_gather | solution.py:85
  149.4 8.8 %fusion.43 = f32[128,1152]{0,1:T(8,128)S(1)} fusion(bf16[128,6144]{1,0:T(8,128)(2,1)S(1)} %fusion.4, bf16[6144,1152]{1,0:T(8,128)(2,1)} %all-gather.6.cloned.1.call-done), kind=kOutput, calls=%fused_computation.74 | convolution fusion | flops 1811939328 | bytes 16318464 | tf_op jit(solution)/shard_map/dot_general | solution.py:83
  158.3 0.3 fusion.38
  158.8 0.7 multiply_reduce_fusion.1
  159.5 75.8 %all-reduce = (f32[]{:T(128)}, f32[]{:T(128)}) all-reduce(f32[]{:T(128)S(6)} %mul.113, f32[]{:T(128)} %multiply_reduce_fusion.1), channel_id=1, replica_groups=mesh['dp'=32,'mp'=8] {'dp','mp'}, use_global_device_ids=true, to_apply=%region_8.9 | all-reduce | flops 2 | bytes 16 | tf_op jit(solution)/shard_map/psum | solution.py:97
  235.3 0.7 divide_convert_fusion
  235.9 0.2 fusion.26
  236.3 0.2 multiply_reduce_fusion.3
  236.6 0.3 fusion.30
  237.1 0.7 pad_maximum_fusion
  237.9 0.9 copy.22
  238.8 32.2 %all_to_all.19 = bf16[128,32,192]{0,2,1:T(8,128)(2,1)S(1)} all-to-all(bf16[128,32,192]{0,2,1:T(8,128)(2,1)S(1)} %bitcast.97), channel_id=1, replica_groups=mesh['dp'=32,'mp'=8] {'dp'}, dimensions={1} | all-to-all | bytes 3145728 | tf_op jit(solution)/shard_map/all_to_all | solution.py:103
  271.0 1.0 copy.23
  272.0 0.7 reshape.147
  274.0 37.2 %all-gather.8.cloned.1.call-done = bf16[4096,1152]{0,1:T(8,128)(2,1)} async-done(((bf16[128,1152]{0,1:T(8,128)(2,1)}), bf16[4096,1152]{0,1:T(8,128)(2,1)}) %all-gather.8.cloned.1.call-update) | async-done | bytes 9437200 | tf_op jit(solution)/shard_map/all_gather | solution.py:107
  311.2 7.8 %fusion.44 = f32[192,3,384]{2,0,1:T(8,128)} fusion(bf16[4096,192,1]{0,1,2:T(8,128)(2,1)S(1)} %reshape.147, bf16[3,384,4096]{2,1,0:T(8,128)(2,1)} %bitcast.104), kind=kOutput, calls=%fused_computation.75 | convolution fusion | flops 1811939328 | bytes 11894784 | tf_op jit(solution)/shard_map/dot_general | solution.py:105
  (36 shorter events, 1.1 us)
Async XLA Ops:
  7.2 26.8 %copy-start = (bf16[128,588]{0,1:T(8,128)(2,1)S(1)}, bf16[128,588]{0,1:T(8,128)(2,1)}, u32[]{:S(2)}) copy-start(bf16[128,588]{0,1:T(8,128)(2,1)} %param.6) | copy-start | bytes 451588
  7.2 29.9 %copy-start.2 = (bf16[128,384]{1,0:T(8,128)(2,1)S(1)}, bf16[128,384]{1,0:T(8,128)(2,1)}, u32[]{:S(2)}) copy-start(bf16[128,384]{1,0:T(8,128)(2,1)} %param.11) | copy-start | bytes 294916
  7.2 30.0 %copy-start.4 = (s32[8]{0:T(128)S(1)}, s32[8]{0:T(128)}, u32[]{:S(2)}) copy-start(s32[8]{0:T(128)} %param.9) | copy-start | bytes 100
  7.2 31.3 %copy-start.3 = (s32[128]{0:T(128)S(1)}, s32[128]{0:T(128)}, u32[]{:S(2)}) copy-start(s32[128]{0:T(128)} %param.10) | copy-start | bytes 1540
  7.2 64.6 %all-gather.4.cloned.1.call-start = ((), (), s32[]{:S(2)}) async-start(), calls=%async_computation.1 | async-start | bytes 1769472 | tf_op jit(solution)/shard_map/all_gather | solution.py:79
  35.1 114.2 %all-gather.6.cloned.1.call-start = ((), (), s32[]{:S(2)}) async-start(), calls=%async_computation.2 | async-start | bytes 14598144 | tf_op jit(solution)/shard_map/all_gather | solution.py:85
  37.0 274.2 %all-gather.8.cloned.1.call-start = ((), (), s32[]{:S(2)}) async-start(), calls=%async_computation.3 | async-start | bytes 9732096 | tf_op jit(solution)/shard_map/all_gather | solution.py:107
  71.8 3.8 %copy-start.1 = (bf16[128,6144]{1,0:T(8,128)(2,1)S(1)}, bf16[128,6144]{1,0:T(8,128)(2,1)}, u32[]{:S(2)}) copy-start(bf16[128,6144]{1,0:T(8,128)(2,1)} %all-gather.4.cloned.1.call-done) | copy-start | bytes 4718596
Sparse Core Ops, SparseCore 0:
  35.3 36.4 all-gather.3
  74.9 74.4 all-gather.5
  238.0 73.2 all-gather.7
where the time goes:
time: 327 us
  waiting for transfers between devices  144 us (44%)
  blocking collectives  135 us (41%)
  matrix products  19.1 us (6%)
  between operations  17 us (5%)
  other arithmetic  7.46 us (2%)
  local copies, waits for them, and re-layouts  4.62 us (1%)
    psum x1, blocking collectives, local(): lax.psum((squared_sum, local_total * lead_flag), ('dp', 'mp'))  75.8 us
    all_gather x1, waiting for transfers between devices, local(): lax.all_gather(flat_weight, 'dp', axis=0, tiled=True)  73.2 us
    all_gather x1, waiting for transfers between devices, local(): lax.all_gather(grad_rows, 'dp', axis=0, tiled=True)  37.2 us
    all_gather x1, waiting for transfers between devices, local(): embedded = lax.all_gather(own_features, 'mp', axis=1, tiled=True)  33.1 us
    all_to_all x1, blocking collectives, local(): lax.all_to_all(normed, 'dp', split_axis=1, concat_axis=0, tiled=True)  32.2 us
    all_gather x1, blocking collectives, local(): lax.all_gather(embed_weight, 'dp', axis=0, tiled=True)  26.7 us
    dot_general x1, matrix products, local(): jnp.dot(section, lax.all_gather(flat_weight, 'dp', axis=0, tiled=True), p...  8.84 us
    dot_general x1, matrix products, local(): lax.dot_general(section, lax.all_gather(grad_rows, 'dp', axis=0, tiled=Tr...  7.85 us
  transfers between devices with their start and end apart: 3, of which 3 were waited for; matrix products, arithmetic and copies ran while one was open for 3% of the time, Pallas kernels for 0%

commit v1 on v0

v1 whole, which is shorter than its diff:
```python
import functools
import math

import jax
import jax.numpy as jnp
from jax import lax
from jax.experimental import pallas as pl
from jax.experimental.pallas import tpu as pltpu
from jax.sharding import Mesh
from jax.sharding import PartitionSpec as P

HD = 128
KEEP = 96
MOVE = 64
P_SIZE = 588
PAD_P = 640
SHARE = 16
SHARES = KEEP // SHARE
STATS = 16
SEGMENT = 600
SIDE = 4
CHIPS = 16
CORES = 2
N_MP = 8
DP = ("y", "x", "core")
F32 = jnp.float32
BF16 = jnp.bfloat16
VMEM = pl.BlockSpec(memory_space=pltpu.VMEM)
SMEM = pl.BlockSpec(memory_space=pltpu.SMEM)
ROOM = pltpu.CompilerParams(vmem_limit_bytes=48 * 1024 * 1024)


def shift(array, axis, size, step):
    return lax.ppermute(array, axis, [(i, (i + step) % size) for i in range(size)])


def swap(array):
    return lax.ppermute(array, "core", [(0, 1), (1, 0)])


def turn(array, first, step):
    pairs = []
    for y in range(SIDE):
        for x in range(SIDE):
            for core in range(CORES):
                along_x = (core == 0) == first
                to_y = y if along_x else (y + step) % SIDE
                to_x = (x + step) % SIDE if along_x else x
                pairs.append(((y * SIDE + x) * CORES + core, (to_y * SIDE + to_x) * CORES + core))
    return lax.ppermute(array, DP, pairs)


def rows_kept(counts_ref):
    end = jnp.int32(0)
    kept = jnp.int32(0)
    for slot in range(counts_ref.shape[0]):
        end = end + counts_ref[slot]
        kept = jnp.where(end <= KEEP, end, kept)
    return pl.multiple_of(kept, 16), end


def pack_kernel(counts_ref, patch_ref, target_ref, segment_ref, embed_ref, all_ref, leave_ref, wide_ref, tall):
    p_size, rows = patch_ref.shape
    tall[...] = jnp.zeros_like(tall)
    tall[:p_size, :] = patch_ref[...].astype(F32)
    marks = jnp.broadcast_to(segment_ref[...].astype(F32) + 1.0, (8, rows))
    tall[SEGMENT : SEGMENT + 8, :] = marks
    all_ref[:rows, :PAD_P] = tall[...].T.astype(BF16)
    all_ref[:rows, PAD_P:] = target_ref[...]
    all_ref[rows:, :] = jnp.zeros((all_ref.shape[0] - rows, all_ref.shape[1]), BF16)
    kept, total = rows_kept(counts_ref)
    leave_ref[...] = all_ref[pl.ds(kept, MOVE), :]
    row = lax.broadcasted_iota(jnp.int32, (wide_ref.shape[0], wide_ref.shape[1] - 512), 0)
    column = lax.broadcasted_iota(jnp.int32, (wide_ref.shape[0], wide_ref.shape[1] - 512), 1)
    here = (row == 0) & (column == p_size - 512)
    wide_ref[:, 512:] = jnp.where(here, total.astype(F32), 0.0).astype(BF16)
    wide_ref[:, :p_size] = embed_ref[...]


def pack(patches, targets, segment_ids, patch_counts, embed_weight):
    rows, p_size = patches.shape
    width = PAD_P + targets.shape[1]
    return pl.pallas_call(
        pack_kernel,
        out_shape=(
            jax.ShapeDtypeStruct((rows + MOVE, width), BF16),
            jax.ShapeDtypeStruct((MOVE, width), BF16),
            jax.ShapeDtypeStruct((embed_weight.shape[0], PAD_P), BF16),
        ),
        grid=(1,),
        in_specs=[SMEM]
        + [
            pl.BlockSpec(shape, lambda i: (0, 0))
            for shape in ((p_size, rows), targets.shape, (1, rows), embed_weight.shape)
        ],
        out_specs=tuple(
            pl.BlockSpec(shape, lambda i: (0, 0))
            for shape in ((rows + MOVE, width), (MOVE, width), (embed_weight.shape[0], PAD_P))
        ),
        scratch_shapes=[pltpu.VMEM((PAD_P, rows), F32)],
        compiler_params=ROOM,
        cost_estimate=pl.CostEstimate(flops=1_000_000, bytes_accessed=1_000_000, transcendentals=0),
    )(patch_counts, patches.T, targets, segment_ids.reshape(1, rows), embed_weight)


def embed_kernel(counts_ref, all_ref, come_ref, wide_ref, out_ref, target_ref, column_ref, row_ref, total_ref, around):
    kept, _ = rows_kept(counts_ref)
    around[...] = jnp.zeros_like(around)
    around[pl.ds(kept, MOVE), :] = come_ref[...]
    mine = lax.broadcasted_iota(jnp.int32, (KEEP, 1), 0) < kept
    merged = jnp.where(mine, all_ref[:KEEP, :], around[:KEEP, :])
    target_ref[...] = merged[:, PAD_P:]
    marks = merged[:, PAD_P - 128 : PAD_P].astype(F32)
    slot = lax.broadcasted_iota(jnp.int32, marks.shape, 1) == SEGMENT - (PAD_P - 128)
    mark = jnp.sum(jnp.where(slot, marks, 0.0), axis=1, keepdims=True) - 1.0
    spread = jnp.broadcast_to(mark, marks.shape)
    column_ref[...] = spread.astype(jnp.int32)
    row_ref[...] = spread.T[:8, :].astype(jnp.int32)
    tail = wide_ref[:, PAD_P - 128 : PAD_P].astype(F32)
    slot = lax.broadcasted_iota(jnp.int32, tail.shape, 1) == P_SIZE - (PAD_P - 128)
    total_ref[...] = jnp.full(total_ref.shape, jnp.sum(jnp.where(slot, tail, 0.0)), F32)
    out_ref[...] = dot_t(merged[:, :PAD_P], wide_ref[...]).astype(BF16)


def embed(patch_counts, packed, coming, wide):
    targets = packed.shape[1] - PAD_P
    return pl.pallas_call(
        embed_kernel,
        out_shape=(
            jax.ShapeDtypeStruct((KEEP, wide.shape[0]), BF16),
            jax.ShapeDtypeStruct((KEEP, targets), BF16),
            jax.ShapeDtypeStruct((KEEP, 128), jnp.int32),
            jax.ShapeDtypeStruct((8, KEEP), jnp.int32),
            jax.ShapeDtypeStruct((8, 128), F32),
        ),
        in_specs=[SMEM] + [VMEM] * 3,
        out_specs=(VMEM,) * 5,
        scratch_shapes=[pltpu.VMEM((KEEP + MOVE, packed.shape[1]), BF16)],
        compiler_params=ROOM,
        cost_estimate=pl.CostEstimate(
            flops=100_000_000, bytes_accessed=2_000_000, transcendentals=0
        ),
    )(patch_counts, packed, coming, wide)


def by_parity(values):
    part = [values[:, 128 * i : 128 * (i + 1)] for i in range(6)]
    turned = [pltpu.roll(p, 64, 1) for p in part]
    low = lax.broadcasted_iota(jnp.int32, part[0].shape, 1) < 64
    even = [part[0], jnp.where(low, part[1], turned[3]), jnp.where(low, turned[3], turned[4])]
    odd = [jnp.where(low, turned[1], turned[2]), jnp.where(low, turned[2], part[4]), part[5]]
    return jnp.concatenate(even, axis=1), jnp.concatenate(odd, axis=1)


def norm_kernel(place_ref, *refs):
    blocks, (share_ref, own_ref, other_ref, chips_ref) = refs[:-4], refs[-4:]
    me, core = place_ref[0], place_ref[1]
    width = blocks[0].shape[1]
    values = [b[...].astype(F32) for b in blocks[:-2]]
    values.append(jnp.concatenate([blocks[-2][...], blocks[-1][...]], axis=0).astype(F32))
    offsets = [0]
    for step in range(1, N_MP // 2):
        offsets += [-step, step]
    offsets.append(N_MP // 2)
    features = width * N_MP
    mean = sum(jnp.sum(v, axis=1, keepdims=True) for v in values) / features
    spread = sum(jnp.sum((v - mean) * (v - mean), axis=1, keepdims=True) for v in values)
    scale = lax.rsqrt(spread / features + 1e-06)
    half = width // 2
    for offset, v in zip(offsets, values):
        place = lax.rem(me + offset + N_MP, N_MP)
        normed = (v - mean) * scale
        chips_ref[2 * place] = normed[:, :half].astype(BF16)
        chips_ref[2 * place + 1] = normed[:, half:].astype(BF16)
        even, odd = by_parity(normed)
        first = core == 0
        columns = pl.ds(pl.multiple_of(place * half, 128), half)
        own_ref[:, columns] = jnp.where(first, even, odd).astype(BF16)
        other_ref[:, columns] = jnp.where(first, odd, even).astype(BF16)
    start = pl.multiple_of(jnp.minimum(me, SHARES - 1) * SHARE, SHARE)
    share_ref[...] = chips_ref[:, pl.ds(start, SHARE), :]


def gather_norm(own, place):
    blocks = [own]
    ahead = back = own
    for _ in range(1, N_MP // 2):
        ahead = shift(ahead, "mp", N_MP, 1)
        back = shift(back, "mp", N_MP, -1)
        blocks += [ahead, back]
    half = own.shape[0] // 2
    blocks.append(shift(ahead[:half], "mp", N_MP, 1))
    blocks.append(shift(back[half:], "mp", N_MP, -1))
    rows, width = own.shape
    return pl.pallas_call(
        norm_kernel,
        out_shape=(
            jax.ShapeDtypeStruct((2 * N_MP, SHARE, width // 2), BF16),
            jax.ShapeDtypeStruct((rows, width * N_MP // 2), BF16),
            jax.ShapeDtypeStruct((rows, width * N_MP // 2), BF16),
        ),
        in_specs=[SMEM] + [VMEM] * len(blocks),
        out_specs=(VMEM, VMEM, VMEM),
        scratch_shapes=[pltpu.VMEM((2 * N_MP, rows, width // 2), BF16)],
        compiler_params=ROOM,
        cost_estimate=pl.CostEstimate(flops=4_000_000, bytes_accessed=4_000_000, transcendentals=0),
    )(place, *blocks)


def project_kernel(own_ref, other_ref, weight_ref, own_out, other_out):
    @pl.when(pl.program_id(0) == 0)
    def _():
        own_out[...] = jnp.zeros_like(own_out)
        other_out[...] = jnp.zeros_like(other_out)

    rows = own_ref.shape[0]
    chips, groups = weight_ref.shape[:2]
    left = jnp.concatenate([own_ref[...], other_ref[...]], axis=0)
    right = jnp.concatenate(
        [
            jnp.concatenate([weight_ref[i, group] for group in range(groups)], axis=1)
            for i in range(chips)
        ],
        axis=0,
    )
    product = jnp.dot(left, right, preferred_element_type=F32)
    own_out[...] += product[:rows]
    other_out[...] += product[rows:]


def project(own, other, weight):
    rows = own.shape[0]
    chips, groups, depth, span = weight.shape
    step = 4
    block = pl.BlockSpec((rows, step * depth), lambda i: (0, i))
    result = pl.BlockSpec((rows, groups * span), lambda i: (0, 0))
    return pl.pallas_call(
        project_kernel,
        grid=(chips // step,),
        out_shape=(jax.ShapeDtypeStruct((rows, groups * span), F32),) * 2,
        in_specs=[
            block,
            block,
            pl.BlockSpec((step, groups, depth, span), lambda i: (i, 0, 0, 0)),
        ],
        out_specs=(result, result),
        compiler_params=ROOM,
        cost_estimate=pl.CostEstimate(
            flops=1_360_000_000, bytes_accessed=9_000_000, transcendentals=0
        ),
    )(own, other, weight)


def dot_t(a, b):
    return lax.dot_general(a, b, (((1,), (1,)), ((), ())), preferred_element_type=F32)


def t_dot(a, b):
    return lax.dot_general(a, b, (((0,), (0,)), ((), ())), preferred_element_type=F32)


def norm_parts(values):
    center = values - jnp.mean(values, axis=-1, keepdims=True)
    scale = lax.rsqrt(jnp.mean(center * center, axis=-1, keepdims=True) + 1e-06)
    return center * scale, scale


def norm_grad(normed, scale, cotangent):
    along = jnp.mean(cotangent * normed, axis=-1, keepdims=True)
    return scale * (cotangent - jnp.mean(cotangent, axis=-1, keepdims=True) - normed * along)


def attend_kernel(raw_ref, more_ref, row_ref, column_ref, target_ref, total_ref, grad_ref):
    inverse_root = 1.0 / math.sqrt(HD)
    heads = target_ref.shape[1] // HD
    rows = raw_ref.shape[0]
    row_segment = row_ref[:, :1]
    valid = row_segment >= 0
    allowed = (row_segment == column_ref[:1, :]) & valid
    total = total_ref[:1, :1]
    squares = jnp.zeros((raw_ref.shape[0], HD), F32)
    for head in range(heads):
        cut = [slice((part * heads + head) * HD, (part * heads + head + 1) * HD) for part in range(3)]
        query, key, value = [raw_ref[:, c] + more_ref[:, c] for c in cut]
        query_exact, query_scale = norm_parts(query)
        key_exact, key_scale = norm_parts(key)
        query_normed = query_exact.astype(BF16)
        key_normed = key_exact.astype(BF16)
        value_rows = value.astype(BF16)
        scores = dot_t(query_normed, key_normed) * inverse_root
        exponent = jnp.where(allowed, jnp.exp(scores), 0.0)
        denominator = jnp.sum(exponent, axis=-1, keepdims=True)
        denominator = jnp.where(valid, denominator, 1.0)
        weights = (exponent / denominator).astype(BF16)
        attended = jnp.dot(weights, value_rows, preferred_element_type=F32)
        target = target_ref[:, head * HD : (head + 1) * HD].astype(F32)
        error = jnp.where(valid, attended - target, 0.0)
        squares += error * error
        out_grad = (error / total).astype(BF16)
        prob_grad = dot_t(out_grad, value_rows)
        grad_ref[:rows, cut[2]] = t_dot(weights, out_grad).astype(BF16)
        weight_float = weights.astype(F32)
        inner = jnp.sum(prob_grad * weight_float, axis=-1, keepdims=True)
        score_grad = (weight_float * (prob_grad - inner) * inverse_root).astype(BF16)
        query_cotangent = jnp.dot(score_grad, key_normed, preferred_element_type=F32)
        key_cotangent = t_dot(score_grad, query_normed)
        grad_ref[:rows, cut[0]] = norm_grad(query_exact, query_scale, query_cotangent).astype(BF16)
        grad_ref[:rows, cut[1]] = norm_grad(key_exact, key_scale, key_cotangent).astype(BF16)
    square = jnp.full((STATS, grad_ref.shape[1]), jnp.sum(squares), F32)
    high = square.astype(BF16).astype(F32)
    middle = (square - high).astype(BF16).astype(F32)
    low = square - high - middle
    place = lax.broadcasted_iota(jnp.int32, square.shape, 0)
    terms = jnp.where(place == 0, high, jnp.where(place == 1, middle, low))
    grad_ref[rows:, :] = jnp.where(place < 3, terms, 0.0).astype(BF16)


def attend(raw, more, column, row, targets, patch_total):
    rows, width = raw.shape
    return pl.pallas_call(
        attend_kernel,
        out_shape=jax.ShapeDtypeStruct((rows + STATS, width), BF16),
        in_specs=[VMEM] * 6,
        out_specs=VMEM,
        compiler_params=ROOM,
        cost_estimate=pl.CostEstimate(
            flops=50_000_000, bytes_accessed=1_500_000, transcendentals=30_000
        ),
    )(raw, more, column, row, targets, patch_total)


def turn_kernel(place_ref, blocks_ref, own_ref, other_ref):
    y, x, core = place_ref[0], place_ref[1], place_ref[2]
    half = blocks_ref.shape[3] // 2
    rows = SHARES * SHARE
    ring = (0, -1, 1, 2)
    pieces = []
    for far in ring:
        for near in ring:
            step_x = jnp.where(core == 0, near, far)
            step_y = jnp.where(core == 0, far, near)
            chip = lax.rem(y + step_y + SIDE, SIDE) * SIDE + lax.rem(x + step_x + SIDE, SIDE)
            pieces += [blocks_ref[share, chip] for share in range(SHARES)]
    for group in range(SIDE):
        several = pieces[group * SIDE * SHARES : (group + 1) * SIDE * SHARES]
        wide = jnp.concatenate(several, axis=0).astype(F32).T.astype(BF16)
        columns = slice(group * SIDE * rows, (group + 1) * SIDE * rows)
        first = core == 0
        own_ref[:, columns] = jnp.where(first, wide[:half], wide[half:])
        other_ref[:, columns] = jnp.where(first, wide[half:], wide[:half])


def turn_blocks(blocks, place):
    _, chips, _, feats = blocks.shape
    return pl.pallas_call(
        turn_kernel,
        out_shape=(jax.ShapeDtypeStruct((feats // 2, chips * KEEP), BF16),) * 2,
        in_specs=[SMEM, VMEM],
        out_specs=(VMEM, VMEM),
        compiler_params=ROOM,
        cost_estimate=pl.CostEstimate(flops=1_000_000, bytes_accessed=2_400_000, transcendentals=0),
    )(place, blocks)


def grad_kernel(parts, own_ref, other_ref, *refs):
    pieces, (own_out, other_out) = refs[:parts], refs[parts:]
    for left_ref, out_ref in ((other_ref, other_out), (own_ref, own_out)):
        groups, _, span = out_ref.shape
        total = None
        start = 0
        for piece in pieces:
            rows = piece.shape[0]
            product = jnp.dot(
                left_ref[:, start : start + rows], piece[...], preferred_element_type=F32
            )
            total = product if total is None else total + product
            start += rows
        for group in range(groups):
            out_ref[group] = total[:, group * span : (group + 1) * span]


def grad_first(own, other, pieces, groups):
    width = pieces[0].shape[1]
    part = jax.ShapeDtypeStruct((groups, own.shape[0], width // groups), F32)
    return pl.pallas_call(
        functools.partial(grad_kernel, len(pieces)),
        out_shape=(part, part),
        in_specs=[VMEM] * (2 + len(pieces)),
        out_specs=(VMEM, VMEM),
        compiler_params=ROOM,
        cost_estimate=pl.CostEstimate(
            flops=1_000_000_000, bytes_accessed=5_000_000, transcendentals=0
        ),
    )(own, other, *pieces)


def last_kernel(start, left_ref, piece_ref, part_ref, out_ref):
    rows = piece_ref.shape[0]
    product = jnp.dot(
        left_ref[:, start : start + rows], piece_ref[...], preferred_element_type=F32
    )
    groups, _, span = out_ref.shape
    for group in range(groups):
        out_ref[group] = part_ref[group] + product[:, group * span : (group + 1) * span]


def grad_last(left, piece, part):
    return pl.pallas_call(
        functools.partial(last_kernel, left.shape[1] - piece.shape[0]),
        out_shape=jax.ShapeDtypeStruct(part.shape, F32),
        in_specs=[VMEM] * 3,
        out_specs=VMEM,
        compiler_params=ROOM,
        cost_estimate=pl.CostEstimate(
            flops=170_000_000, bytes_accessed=3_000_000, transcendentals=0
        ),
    )(left, piece, part)


def add_kernel(a_ref, b_ref, out_ref):
    out_ref[...] = a_ref[...] + b_ref[...]


def add(a, b):
    return pl.pallas_call(
        add_kernel,
        out_shape=jax.ShapeDtypeStruct(a.shape, F32),
        in_specs=[VMEM, VMEM],
        out_specs=VMEM,
        compiler_params=ROOM,
    )(a, b)


def near_kernel(*refs):
    blocks, (out_ref, sum_ref) = refs[:-2], refs[-2:]
    rows = blocks[0].shape[0] - STATS
    terms = 0.0
    for index, block in enumerate(blocks):
        out_ref[index * rows : (index + 1) * rows, :] = block[:rows, :]
        terms += block[rows:, :128].astype(F32)
    sum_ref[...] = jnp.broadcast_to(jnp.sum(terms, axis=0, keepdims=True), sum_ref.shape)


def near_rows(blocks):
    rows, width = blocks[0].shape
    return pl.pallas_call(
        near_kernel,
        out_shape=(
            jax.ShapeDtypeStruct((len(blocks) * (rows - STATS), width), BF16),
            jax.ShapeDtypeStruct((8, 128), F32),
        ),
        in_specs=[VMEM] * len(blocks),
        out_specs=(VMEM, VMEM),
        compiler_params=ROOM,
        cost_estimate=pl.CostEstimate(flops=100_000, bytes_accessed=1_800_000, transcendentals=0),
    )(*blocks)


def local(patches, embed_weight, project_weight, patch_counts, segment_ids, targets):
    whole_weight = lax.all_gather(project_weight.transpose(1, 0, 2), ("y", "x"), axis=0)
    y, x, core, mp = [lax.axis_index(a) for a in ("y", "x", "core", "mp")]

    packed, leaving, embed_part = pack(patches, targets, segment_ids, patch_counts, embed_weight)
    half = CHIPS * CORES // 2
    coming = lax.ppermute(leaving, DP, [(i + half, i) for i in range(half)])
    wide = lax.all_gather(embed_part, DP, axis=0, tiled=True)
    own_features, targets, column, row, total_tile = embed(patch_counts, packed, coming, wide)
    chip_blocks, own_half, other_half = gather_norm(own_features, jnp.stack([mp, core]))
    chip_share = lax.all_to_all(chip_blocks, ("y", "x"), split_axis=0, concat_axis=0, tiled=True)
    more_half, chip_share = lax.optimization_barrier((swap(other_half), chip_share))
    chip_rows = lax.all_gather(chip_share, "mp", axis=0)
    own_part, other_part = project(own_half, more_half, whole_weight)
    grad_rows = attend(own_part, swap(other_part), column, row, targets, total_tile)

    behind, ahead = lax.optimization_barrier(
        (turn(grad_rows, True, 1), turn(grad_rows, True, -1))
    )
    near, tile = near_rows([grad_rows, behind, ahead, turn(behind, True, 1)])
    own_left, other_left = turn_blocks(chip_rows, jnp.stack([y, x, core]))
    behind, ahead = turn(near, False, 1), turn(near, False, -1)
    for step in (1, 2, 4):
        tile = tile + shift(tile, "mp", N_MP, step)
    behind, ahead, tile, own_left, other_left = lax.optimization_barrier(
        (behind, ahead, tile, own_left, other_left)
    )
    groups = project_weight.shape[1]
    own_grad, other_grad = grad_first(own_left, other_left, (near, behind, ahead), groups)
    opposite = turn(behind, False, 1)
    for step in (-1, -2):
        tile = tile + turn(tile, False, step)
    opposite, tile, own_grad, other_grad = lax.optimization_barrier(
        (opposite, tile, own_grad, other_grad)
    )
    more_grad, more_tile = lax.optimization_barrier(
        (swap(grad_last(other_left, opposite, other_grad)), swap(tile))
    )
    weight_grad = add(grad_last(own_left, opposite, own_grad), more_grad)
    loss_value = (tile + more_tile)[0, 0] / (2.0 * total_tile[0, 0])
    return (weight_grad.transpose(1, 0, 2), loss_value)


def solution(mesh):
    chips = Mesh(mesh.devices.reshape(SIDE, SIDE, CORES, N_MP), DP + ("mp",))
    in_specs = (
        P(DP, None),
        P(("mp",) + DP, None),
        P(DP, None, "mp"),
        P(DP),
        P(DP),
        P(DP, "mp"),
    )
    out_specs = (P(DP, None, "mp"), P())
    return jax.shard_map(
        local, mesh=chips, in_specs=in_specs, out_specs=out_specs, check_vma=False
    )
```

time: 327 us -> 164 us (0.50)
  waiting for transfers between devices: 144 us -> 41.5 us
  blocking collectives: 135 us -> 43.1 us
  starting transfers between devices: 0.12 us -> 40.6 us
  matrix products: 19.1 us -> 0 us
  Pallas kernels: 0 us -> 15.3 us
  other arithmetic: 7.46 us -> 0.17 us
    all_gather x3 -> x2, waiting for transfers between devices: 144 us -> 0.02 us  [the longest x1 0.02 us: local(): lax.all_gather(project_weight.transpose(1, 0, 2), ('y', 'x'), axis=0)]
    psum x1 -> x0, blocking collectives: 75.8 us -> none  [local(): lax.psum((squared_sum, local_total * lead_flag), ('dp', 'mp'))]
    ppermute x0 -> x24, waiting for transfers between devices: none -> 40.7 us  [the longest x11 20.3 us: shift(): lax.ppermute(array, axis, [(i, (i + step) % size) for i in range(size)])]
    ppermute x0 -> x24, starting transfers between devices: none -> 40.5 us  [the longest x11 19 us: shift(): lax.ppermute(array, axis, [(i, (i + step) % size) for i in range(size)])]
    dot_general x9 -> x0, matrix products: 19.1 us -> none  [the longest x1 8.84 us: local(): jnp.dot(section, lax.all_gather(flat_weight, 'dp', axis=0, tiled=True), p...]
    all_to_all x1, blocking collectives: 32.2 us -> 13.8 us  [local(): lax.all_to_all(chip_blocks, ('y', 'x'), split_axis=0, concat_axis=0, tile...]
    pallas_call x0 -> x11, Pallas kernels: none -> 15.3 us  [the longest x1 4.96 us: project(): pl.pallas_call(project_kernel, grid=(chips // step,), out_shape=(jax.Shap...]
    reduce_sum x6 -> x0, other arithmetic: 5.19 us -> none  [the longest x2 2.04 us: layer_norm(): spread = jnp.mean(center * center, axis=-1, keepdims=True)]
  transfers between devices with their start and end apart: 3 -> 26, of which waited for: 3 -> 13; matrix products, arithmetic and copies ran while one was open for 3% -> 0% of each run, Pallas kernels for 0% -> 9%
where the time goes in v1:
time: 164 us
  blocking collectives  43.1 us (26%)
  waiting for transfers between devices  41.5 us (25%)
  starting transfers between devices  40.6 us (25%)
  between operations  16.7 us (10%)
  Pallas kernels  15.3 us (9%)
  local copies, waits for them, and re-layouts  6.31 us (4%)
    all_gather x1, blocking collectives, local(): wide = lax.all_gather(embed_part, DP, axis=0, tiled=True)  29.3 us
    ppermute x11, waiting for transfers between devices, shift(): lax.ppermute(array, axis, [(i, (i + step) % size) for i in range(size)])  20.3 us
    ppermute x11, starting transfers between devices, shift(): lax.ppermute(array, axis, [(i, (i + step) % size) for i in range(size)])  19 us
    ppermute x8, waiting for transfers between devices, turn(): return lax.ppermute(array, DP, pairs)  18.3 us
    all_to_all x1, blocking collectives, local(): lax.all_to_all(chip_blocks, ('y', 'x'), split_axis=0, concat_axis=0, tile...  13.8 us
    ppermute x4, starting transfers between devices, swap(): return lax.ppermute(array, 'core', [(0, 1), (1, 0)])  10.3 us
    ppermute x8, starting transfers between devices, turn(): return lax.ppermute(array, DP, pairs)  9.96 us
    unnamed x12, local copies, waits for them, and re-layouts  5.27 us
  transfers between devices with their start and end apart: 26, of which 13 were waited for; matrix products, arithmetic and copies ran while one was open for 0% of the time, Pallas kernels for 9%

profile of v1, /device:TPU:1, one launch (start us, length us, event | category | flops | bytes accessed | tf_op | source)
XLA Modules:
  0.0 163.7 jit_solution(15917483490833002411)
XLA Ops:
  13.8 29.3 %all_gather.15.wide_ref = bf16[768,640]{1,0:T(8,128)(2,1)S(1)} all-gather(bf16[24,640]{1,0:T(8,128)(2,1)S(1)} %get-tuple-element.38), channel_id=1, replica_groups=mesh['y'=4,'x'=4,'core'=2,'mp'=8] {'y','x','core'}, dimensions={0}, use_global_device_ids=true | all-gather | bytes 1013760 | tf_op jit(solution)/shard_map/all_gather | solution.py:466
  45.8 4.1 %collective-permute-start.2 = (bf16[96,768]{1,0:T(8,128)(2,1)S(1)}, bf16[96,768]{1,0:T(8,128)(2,1)S(1)}, u32[]{:S(2)}, u32[]{:S(2)}) collective-permute-start(bf16[96,768]{1,0:T(8,128)(2,1)S(1)} %get-tuple-element.39.refs_0_), channel_id=1, source_target_pairs={{0,7},{1,0},{2,1},{3,2},{4,3},{5,4},{6,5},{7,6},{8,15},{9,8},{10,9... | collective-permute-start | bytes 442376 | tf_op jit(solution)/shard_map/ppermute | solution.py:34
  49.9 4.0 %collective-permute-done.1.refs_1_ = bf16[96,768]{1,0:T(8,128)(2,1)S(1)} collective-permute-done((bf16[96,768]{1,0:T(8,128)(2,1)S(1)}, bf16[96,768]{1,0:T(8,128)(2,1)S(1)}, u32[]{:S(2)}, u32[]{:S(2)}) %collective-permute-start.1) | collective-permute-done | bytes 147488 | tf_op jit(solution)/shard_map/ppermute | solution.py:34
  53.9 2.7 %collective-permute-start.4 = (bf16[96,768]{1,0:T(8,128)(2,1)S(1)}, bf16[96,768]{1,0:T(8,128)(2,1)S(1)}, u32[]{:S(2)}, u32[]{:S(2)}) collective-permute-start(bf16[96,768]{1,0:T(8,128)(2,1)S(1)} %collective-permute-done.2.refs_2_), channel_id=1, source_target_pairs={{0,7},{1,0},{2,1},{3,2},{4,3},{5,4},{6,5},{7,6},{8,15},{9,8},{10,9... | collective-permute-start | bytes 442376 | tf_op jit(solution)/shard_map/ppermute | solution.py:34
  56.5 3.3 %collective-permute-done.3.refs_3_ = bf16[96,768]{1,0:T(8,128)(2,1)S(1)} collective-permute-done((bf16[96,768]{1,0:T(8,128)(2,1)S(1)}, bf16[96,768]{1,0:T(8,128)(2,1)S(1)}, u32[]{:S(2)}, u32[]{:S(2)}) %collective-permute-start.3) | collective-permute-done | bytes 147488 | tf_op jit(solution)/shard_map/ppermute | solution.py:34
  59.8 2.7 %collective-permute-start.6 = (bf16[96,768]{1,0:T(8,128)(2,1)S(1)}, bf16[96,768]{1,0:T(8,128)(2,1)S(1)}, u32[]{:S(2)}, u32[]{:S(2)}) collective-permute-start(bf16[96,768]{1,0:T(8,128)(2,1)S(1)} %collective-permute-done.4.refs_4_), channel_id=1, source_target_pairs={{0,7},{1,0},{2,1},{3,2},{4,3},{5,4},{6,5},{7,6},{8,15},{9,8},{10,9... | collective-permute-start | bytes 442376 | tf_op jit(solution)/shard_map/ppermute | solution.py:34
  62.5 2.9 %collective-permute-done.5.refs_5_ = bf16[96,768]{1,0:T(8,128)(2,1)S(1)} collective-permute-done((bf16[96,768]{1,0:T(8,128)(2,1)S(1)}, bf16[96,768]{1,0:T(8,128)(2,1)S(1)}, u32[]{:S(2)}, u32[]{:S(2)}) %collective-permute-start.5) | collective-permute-done | bytes 147488 | tf_op jit(solution)/shard_map/ppermute | solution.py:34
  65.5 2.7 %collective-permute-start.8 = (bf16[48,768]{1,0:T(8,128)(2,1)S(1)}, bf16[48,768]{1,0:T(8,128)(2,1)S(1)}, u32[]{:S(2)}, u32[]{:S(2)}) collective-permute-start(bf16[48,768]{1,0:T(8,128)(2,1)S(1)} %slice.17), channel_id=1, source_target_pairs={{0,7},{1,0},{2,1},{3,2},{4,3},{5,4},{6,5},{7,6},{8,15},{9,8},{10,9... | collective-permute-start | bytes 221192 | tf_op jit(solution)/shard_map/ppermute | solution.py:34
  68.3 2.0 %collective-permute-done.7.refs_7_ = bf16[48,768]{1,0:T(8,128)(2,1)S(1)} collective-permute-done((bf16[48,768]{1,0:T(8,128)(2,1)S(1)}, bf16[48,768]{1,0:T(8,128)(2,1)S(1)}, u32[]{:S(2)}, u32[]{:S(2)}) %collective-permute-start.7) | collective-permute-done | bytes 73760 | tf_op jit(solution)/shard_map/ppermute | solution.py:34
  70.2 1.8 %shard_map.79 = (bf16[16,16,384]{2,1,0:T(8,128)(2,1)S(1)}, bf16[96,3072]{1,0:T(8,128)(2,1)S(1)}, bf16[96,3072]{1,0:T(8,128)(2,1)S(1)}) custom-call(s32[2]{0:T(128)S(1)} %pad_add_fusion.place_ref, bf16[96,768]{1,0:T(8,128)(2,1)S(1)} %get-tuple-element.39.refs_0_, bf16[96,768]{1,0:T(8,128)(2,1)S(1)} %collective-permute-done.1.refs_1_, ...), custom_call_target="tpu_custom_call" | custom-call | flops 4000000 | bytes 4000000 | tf_op jit(solution)/shard_map/pallas_call | solution.py:195
  72.1 3.1 %collective-permute-start.9 = (bf16[96,3072]{1,0:T(8,128)(2,1)S(1)}, bf16[96,3072]{1,0:T(8,128)(2,1)S(1)}, u32[]{:S(2)}, u32[]{:S(2)}) collective-permute-start(bf16[96,3072]{1,0:T(8,128)(2,1)S(1)} %get-tuple-element.41), channel_id=1, source_target_pairs={{0,8},{8,0},{1,9},{9,1},{2,10},{10,2},{3,11},{11,3},{4,12},{12,4},... | collective-permute-start | bytes 1769480 | tf_op jit(solution)/shard_map/ppermute | solution.py:38
  75.2 13.8 %all_to_all.5 = bf16[16,16,384]{2,1,0:T(8,128)(2,1)} all-to-all(bf16[16,16,384]{2,1,0:T(8,128)(2,1)S(1)} %get-tuple-element.42), channel_id=1, replica_groups=mesh['y'=4,'x'=4,'core'=2,'mp'=8] {'y','x'}, dimensions={0} | all-to-all | bytes 393216 | tf_op jit(solution)/shard_map/all_to_all | solution.py:469
  89.0 5.0 %shard_map.80 = (f32[96,1152]{1,0:T(8,128)S(1)}, f32[96,1152]{1,0:T(8,128)S(1)}) custom-call(bf16[96,3072]{1,0:T(8,128)(2,1)S(1)} %get-tuple-element.40.own_ref, bf16[96,3072]{1,0:T(8,128)(2,1)S(1)} %collective-permute-done.9.other_ref, bf16[16,3,192,384]{3,2,1,0:T(8,128)(2,1)} %bitcast.14), custom_call_target="tpu_custom_call" | custom-call | flops 1360000000 | bytes 9000000 | tf_op jit(solution)/shard_map/pallas_call | solution.py:237
  96.6 2.4 %shard_map.81.refs_0_ = bf16[112,1152]{1,0:T(8,128)(2,1)S(1)} custom-call(f32[96,1152]{1,0:T(8,128)S(1)} %get-tuple-element.44.raw_ref, f32[96,1152]{1,0:T(8,128)S(1)} %collective-permute-done.10.more_ref, s32[96,128]{1,0:T(8,128)S(1)} %get-tuple-element.46.row_ref, s32[8,96]{1,0:T(8,128)S(1)} %get-tuple-element.47.column_ref, ...), custom_call_target="tpu_custom_call" | custom-call | flops 50000000 | bytes 1500000 | tf_op jit(solution)/shard_map/pallas_call | solution.py:320
  99.2 2.7 %collective-permute-start.12 = (bf16[112,1152]{1,0:T(8,128)(2,1)S(1)}, bf16[112,1152]{1,0:T(8,128)(2,1)S(1)}, u32[]{:S(2)}, u32[]{:S(2)}) collective-permute-start(bf16[112,1152]{1,0:T(8,128)(2,1)S(1)} %shard_map.81.refs_0_), channel_id=1, source_target_pairs={{0,48},{8,200},{16,0},{24,216},{32,16},{40,232},{48,32},{56,248},{... | collective-permute-start | bytes 774152 | tf_op jit(solution)/shard_map/ppermute | solution.py:50
  101.8 4.1 %collective-permute-done.11.refs_1_ = bf16[112,1152]{1,0:T(8,128)(2,1)S(1)} collective-permute-done((bf16[112,1152]{1,0:T(8,128)(2,1)S(1)}, bf16[112,1152]{1,0:T(8,128)(2,1)S(1)}, u32[]{:S(2)}, u32[]{:S(2)}) %collective-permute-start.11) | collective-permute-done | bytes 258080 | tf_op jit(solution)/shard_map/ppermute | solution.py:50
  105.9 6.8 %collective-permute-done.13.refs_3_ = bf16[112,1152]{1,0:T(8,128)(2,1)S(1)} collective-permute-done((bf16[112,1152]{1,0:T(8,128)(2,1)S(1)}, bf16[112,1152]{1,0:T(8,128)(2,1)S(1)}, u32[]{:S(2)}, u32[]{:S(2)}) %collective-permute-start.13) | collective-permute-done | bytes 258080 | tf_op jit(solution)/shard_map/ppermute | solution.py:50
  113.2 2.4 %collective-permute-start.15 = (bf16[384,1152]{1,0:T(8,128)(2,1)S(1)}, bf16[384,1152]{1,0:T(8,128)(2,1)S(1)}, u32[]{:S(2)}, u32[]{:S(2)}) collective-permute-start(bf16[384,1152]{1,0:T(8,128)(2,1)S(1)} %get-tuple-element.52.refs_0_), channel_id=1, source_target_pairs={{0,192},{8,56},{16,208},{24,8},{32,224},{40,24},{48,240},{56,40},{... | collective-permute-start | bytes 2654216 | tf_op jit(solution)/shard_map/ppermute | solution.py:50
  115.5 4.2 %collective-permute-done.16 = f32[8,128]{1,0:T(8,128)S(1)} collective-permute-done((f32[8,128]{1,0:T(8,128)S(1)}, f32[8,128]{1,0:T(8,128)S(1)}, u32[]{:S(2)}, u32[]{:S(2)}) %collective-permute-start.16) | collective-permute-done | bytes 4128 | tf_op jit(solution)/shard_map/ppermute | solution.py:34
  120.5 3.9 %collective-permute-done.17 = f32[8,128]{1,0:T(8,128)S(1)} collective-permute-done((f32[8,128]{1,0:T(8,128)S(1)}, f32[8,128]{1,0:T(8,128)S(1)}, u32[]{:S(2)}, u32[]{:S(2)}) %collective-permute-start.17) | collective-permute-done | bytes 4128 | tf_op jit(solution)/shard_map/ppermute | solution.py:34
  124.4 4.4 %collective-permute-start.18 = (f32[8,128]{1,0:T(8,128)S(1)}, f32[8,128]{1,0:T(8,128)S(1)}, u32[]{:S(2)}, u32[]{:S(2)}) collective-permute-start(f32[8,128]{1,0:T(8,128)S(1)} %add.19), channel_id=1, source_target_pairs={{0,4},{1,5},{2,6},{3,7},{4,0},{5,1},{6,2},{7,3},{8,12},{9,13},{10,... | collective-permute-start | bytes 12296 | tf_op jit(solution)/shard_map/ppermute | solution.py:34
  131.4 2.7 %collective-permute-start.20 = (f32[8,128]{1,0:T(8,128)S(1)}, f32[8,128]{1,0:T(8,128)S(1)}, u32[]{:S(2)}, u32[]{:S(2)}) collective-permute-start(f32[8,128]{1,0:T(8,128)S(1)} %add.20), channel_id=1, source_target_pairs={{0,192},{8,56},{16,208},{24,8},{32,224},{40,24},{48,240},{56,40},{... | collective-permute-start | bytes 12296 | tf_op jit(solution)/shard_map/ppermute | solution.py:50
  138.2 5.2 %collective-permute-done.21 = f32[8,128]{1,0:T(8,128)S(1)} collective-permute-done((f32[8,128]{1,0:T(8,128)S(1)}, f32[8,128]{1,0:T(8,128)S(1)}, u32[]{:S(2)}, u32[]{:S(2)}) %collective-permute-start.21) | collective-permute-done | bytes 4128 | tf_op jit(solution)/shard_map/ppermute | solution.py:50
  145.2 5.9 %collective-permute-start.22 = (f32[3,192,384]{2,1,0:T(8,128)S(1)}, f32[3,192,384]{2,1,0:T(8,128)S(1)}, u32[]{:S(2)}, u32[]{:S(2)}) collective-permute-start(f32[3,192,384]{2,1,0:T(8,128)S(1)} %shard_map.86), channel_id=1, source_target_pairs={{0,8},{8,0},{1,9},{9,1},{2,10},{10,2},{3,11},{11,3},{4,12},{12,4},... | collective-permute-start | bytes 2654216 | tf_op jit(solution)/shard_map/ppermute | solution.py:38
  (67 shorter events, 25.1 us)
Async XLA Ops:
  7.2 81.9 %all-gather.5.cloned.1.call-start = ((), (), s32[]{:S(2)}) async-start(), calls=%async_computation.1 | async-start | bytes 7520256 | tf_op jit(solution)/shard_map/all_gather | solution.py:460
  7.9 121.0 %all-gather.7.cloned.1.call-start = ((), (), s32[]{:S(2)}) async-start(), calls=%async_computation.2 | async-start | bytes 1769472 | tf_op jit(solution)/shard_map/all_gather | solution.py:471
  12.5 30.6 %collective-permute-start = (bf16[64,1024]{1,0:T(8,128)(2,1)S(1)}, bf16[64,1024]{1,0:T(8,128)(2,1)S(1)}, u32[]{:S(2)}, u32[]{:S(2)}) collective-permute-start(bf16[64,1024]{1,0:T(8,128)(2,1)S(1)} %get-tuple-element.37), channel_id=1, source_target_pairs={{128,0},{136,8},{144,16},{152,24},{160,32},{168,40},{176,48},{184,... | collective-permute-start | bytes 393224 | tf_op jit(solution)/shard_map/ppermute | solution.py:465
  44.1 9.7 %collective-permute-start.1 = (bf16[96,768]{1,0:T(8,128)(2,1)S(1)}, bf16[96,768]{1,0:T(8,128)(2,1)S(1)}, u32[]{:S(2)}, u32[]{:S(2)}) collective-permute-start(bf16[96,768]{1,0:T(8,128)(2,1)S(1)} %get-tuple-element.39.refs_0_), channel_id=1, source_target_pairs={{0,1},{1,2},{2,3},{3,4},{4,5},{5,6},{6,7},{7,0},{8,9},{9,10},{10,1... | collective-permute-start | bytes 442376 | tf_op jit(solution)/shard_map/ppermute | solution.py:34
  45.8 8.1 %collective-permute-start.2 = (bf16[96,768]{1,0:T(8,128)(2,1)S(1)}, bf16[96,768]{1,0:T(8,128)(2,1)S(1)}, u32[]{:S(2)}, u32[]{:S(2)}) collective-permute-start(bf16[96,768]{1,0:T(8,128)(2,1)S(1)} %get-tuple-element.39.refs_0_), channel_id=1, source_target_pairs={{0,7},{1,0},{2,1},{3,2},{4,3},{5,4},{6,5},{7,6},{8,15},{9,8},{10,9... | collective-permute-start | bytes 442376 | tf_op jit(solution)/shard_map/ppermute | solution.py:34
  53.9 6.0 %collective-permute-start.3 = (bf16[96,768]{1,0:T(8,128)(2,1)S(1)}, bf16[96,768]{1,0:T(8,128)(2,1)S(1)}, u32[]{:S(2)}, u32[]{:S(2)}) collective-permute-start(bf16[96,768]{1,0:T(8,128)(2,1)S(1)} %collective-permute-done.1.refs_1_), channel_id=1, source_target_pairs={{0,1},{1,2},{2,3},{3,4},{4,5},{5,6},{6,7},{7,0},{8,9},{9,10},{10,1... | collective-permute-start | bytes 442376 | tf_op jit(solution)/shard_map/ppermute | solution.py:34
  53.9 6.0 %collective-permute-start.4 = (bf16[96,768]{1,0:T(8,128)(2,1)S(1)}, bf16[96,768]{1,0:T(8,128)(2,1)S(1)}, u32[]{:S(2)}, u32[]{:S(2)}) collective-permute-start(bf16[96,768]{1,0:T(8,128)(2,1)S(1)} %collective-permute-done.2.refs_2_), channel_id=1, source_target_pairs={{0,7},{1,0},{2,1},{3,2},{4,3},{5,4},{6,5},{7,6},{8,15},{9,8},{10,9... | collective-permute-start | bytes 442376 | tf_op jit(solution)/shard_map/ppermute | solution.py:34
  59.8 5.6 %collective-permute-start.5 = (bf16[96,768]{1,0:T(8,128)(2,1)S(1)}, bf16[96,768]{1,0:T(8,128)(2,1)S(1)}, u32[]{:S(2)}, u32[]{:S(2)}) collective-permute-start(bf16[96,768]{1,0:T(8,128)(2,1)S(1)} %collective-permute-done.3.refs_3_), channel_id=1, source_target_pairs={{0,1},{1,2},{2,3},{3,4},{4,5},{5,6},{6,7},{7,0},{8,9},{9,10},{10,1... | collective-permute-start | bytes 442376 | tf_op jit(solution)/shard_map/ppermute | solution.py:34
  59.8 5.6 %collective-permute-start.6 = (bf16[96,768]{1,0:T(8,128)(2,1)S(1)}, bf16[96,768]{1,0:T(8,128)(2,1)S(1)}, u32[]{:S(2)}, u32[]{:S(2)}) collective-permute-start(bf16[96,768]{1,0:T(8,128)(2,1)S(1)} %collective-permute-done.4.refs_4_), channel_id=1, source_target_pairs={{0,7},{1,0},{2,1},{3,2},{4,3},{5,4},{6,5},{7,6},{8,15},{9,8},{10,9... | collective-permute-start | bytes 442376 | tf_op jit(solution)/shard_map/ppermute | solution.py:34
  65.4 4.8 %collective-permute-start.7 = (bf16[48,768]{1,0:T(8,128)(2,1)S(1)}, bf16[48,768]{1,0:T(8,128)(2,1)S(1)}, u32[]{:S(2)}, u32[]{:S(2)}) collective-permute-start(bf16[48,768]{1,0:T(8,128)(2,1)S(1)} %slice.16), channel_id=1, source_target_pairs={{0,1},{1,2},{2,3},{3,4},{4,5},{5,6},{6,7},{7,0},{8,9},{9,10},{10,1... | collective-permute-start | bytes 221192 | tf_op jit(solution)/shard_map/ppermute | solution.py:34
  65.5 4.8 %collective-permute-start.8 = (bf16[48,768]{1,0:T(8,128)(2,1)S(1)}, bf16[48,768]{1,0:T(8,128)(2,1)S(1)}, u32[]{:S(2)}, u32[]{:S(2)}) collective-permute-start(bf16[48,768]{1,0:T(8,128)(2,1)S(1)} %slice.17), channel_id=1, source_target_pairs={{0,7},{1,0},{2,1},{3,2},{4,3},{5,4},{6,5},{7,6},{8,15},{9,8},{10,9... | collective-permute-start | bytes 221192 | tf_op jit(solution)/shard_map/ppermute | solution.py:34
  72.1 16.9 %collective-permute-start.9 = (bf16[96,3072]{1,0:T(8,128)(2,1)S(1)}, bf16[96,3072]{1,0:T(8,128)(2,1)S(1)}, u32[]{:S(2)}, u32[]{:S(2)}) collective-permute-start(bf16[96,3072]{1,0:T(8,128)(2,1)S(1)} %get-tuple-element.41), channel_id=1, source_target_pairs={{0,8},{8,0},{1,9},{9,1},{2,10},{10,2},{3,11},{11,3},{4,12},{12,4},... | collective-permute-start | bytes 1769480 | tf_op jit(solution)/shard_map/ppermute | solution.py:38
  99.1 6.9 %collective-permute-start.11 = (bf16[112,1152]{1,0:T(8,128)(2,1)S(1)}, bf16[112,1152]{1,0:T(8,128)(2,1)S(1)}, u32[]{:S(2)}, u32[]{:S(2)}) collective-permute-start(bf16[112,1152]{1,0:T(8,128)(2,1)S(1)} %shard_map.81.refs_0_), channel_id=1, source_target_pairs={{0,16},{8,72},{16,32},{24,88},{32,48},{40,104},{48,0},{56,120},{64... | collective-permute-start | bytes 774152 | tf_op jit(solution)/shard_map/ppermute | solution.py:50
  99.2 6.8 %collective-permute-start.12 = (bf16[112,1152]{1,0:T(8,128)(2,1)S(1)}, bf16[112,1152]{1,0:T(8,128)(2,1)S(1)}, u32[]{:S(2)}, u32[]{:S(2)}) collective-permute-start(bf16[112,1152]{1,0:T(8,128)(2,1)S(1)} %shard_map.81.refs_0_), channel_id=1, source_target_pairs={{0,48},{8,200},{16,0},{24,216},{32,16},{40,232},{48,32},{56,248},{... | collective-permute-start | bytes 774152 | tf_op jit(solution)/shard_map/ppermute | solution.py:50
  105.9 6.8 %collective-permute-start.13 = (bf16[112,1152]{1,0:T(8,128)(2,1)S(1)}, bf16[112,1152]{1,0:T(8,128)(2,1)S(1)}, u32[]{:S(2)}, u32[]{:S(2)}) collective-permute-start(bf16[112,1152]{1,0:T(8,128)(2,1)S(1)} %collective-permute-done.11.refs_1_), channel_id=1, source_target_pairs={{0,16},{8,72},{16,32},{24,88},{32,48},{40,104},{48,0},{56,120},{64... | collective-permute-start | bytes 774152 | tf_op jit(solution)/shard_map/ppermute | solution.py:50
  112.8 18.5 %collective-permute-start.14 = (bf16[384,1152]{1,0:T(8,128)(2,1)S(1)}, bf16[384,1152]{1,0:T(8,128)(2,1)S(1)}, u32[]{:S(2)}, u32[]{:S(2)}) collective-permute-start(bf16[384,1152]{1,0:T(8,128)(2,1)S(1)} %get-tuple-element.52.refs_0_), channel_id=1, source_target_pairs={{0,64},{8,24},{16,80},{24,40},{32,96},{40,56},{48,112},{56,8},{64,... | collective-permute-start | bytes 2654216 | tf_op jit(solution)/shard_map/ppermute | solution.py:50
  113.2 18.1 %collective-permute-start.15 = (bf16[384,1152]{1,0:T(8,128)(2,1)S(1)}, bf16[384,1152]{1,0:T(8,128)(2,1)S(1)}, u32[]{:S(2)}, u32[]{:S(2)}) collective-permute-start(bf16[384,1152]{1,0:T(8,128)(2,1)S(1)} %get-tuple-element.52.refs_0_), channel_id=1, source_target_pairs={{0,192},{8,56},{16,208},{24,8},{32,224},{40,24},{48,240},{56,40},{... | collective-permute-start | bytes 2654216 | tf_op jit(solution)/shard_map/ppermute | solution.py:50
  115.5 4.2 %collective-permute-start.16 = (f32[8,128]{1,0:T(8,128)S(1)}, f32[8,128]{1,0:T(8,128)S(1)}, u32[]{:S(2)}, u32[]{:S(2)}) collective-permute-start(f32[8,128]{1,0:T(8,128)S(1)} %get-tuple-element.53), channel_id=1, source_target_pairs={{0,1},{1,2},{2,3},{3,4},{4,5},{5,6},{6,7},{7,0},{8,9},{9,10},{10,1... | collective-permute-start | bytes 12296 | tf_op jit(solution)/shard_map/ppermute | solution.py:34
  119.8 4.6 %collective-permute-start.17 = (f32[8,128]{1,0:T(8,128)S(1)}, f32[8,128]{1,0:T(8,128)S(1)}, u32[]{:S(2)}, u32[]{:S(2)}) collective-permute-start(f32[8,128]{1,0:T(8,128)S(1)} %add.18), channel_id=1, source_target_pairs={{0,2},{1,3},{2,4},{3,5},{4,6},{5,7},{6,0},{7,1},{8,10},{9,11},{10,... | collective-permute-start | bytes 12296 | tf_op jit(solution)/shard_map/ppermute | solution.py:34
  124.4 6.9 %collective-permute-start.18 = (f32[8,128]{1,0:T(8,128)S(1)}, f32[8,128]{1,0:T(8,128)S(1)}, u32[]{:S(2)}, u32[]{:S(2)}) collective-permute-start(f32[8,128]{1,0:T(8,128)S(1)} %add.19), channel_id=1, source_target_pairs={{0,4},{1,5},{2,6},{3,7},{4,0},{5,1},{6,2},{7,3},{8,12},{9,13},{10,... | collective-permute-start | bytes 12296 | tf_op jit(solution)/shard_map/ppermute | solution.py:34
  131.3 13.5 %collective-permute-start.19 = (bf16[384,1152]{1,0:T(8,128)(2,1)S(1)}, bf16[384,1152]{1,0:T(8,128)(2,1)S(1)}, u32[]{:S(2)}, u32[]{:S(2)}) collective-permute-start(bf16[384,1152]{1,0:T(8,128)(2,1)S(1)} %collective-permute-done.14.refs_1_), channel_id=1, source_target_pairs={{0,64},{8,24},{16,80},{24,40},{32,96},{40,56},{48,112},{56,8},{64,... | collective-permute-start | bytes 2654216 | tf_op jit(solution)/shard_map/ppermute | solution.py:50
  131.4 3.4 %collective-permute-start.20 = (f32[8,128]{1,0:T(8,128)S(1)}, f32[8,128]{1,0:T(8,128)S(1)}, u32[]{:S(2)}, u32[]{:S(2)}) collective-permute-start(f32[8,128]{1,0:T(8,128)S(1)} %add.20), channel_id=1, source_target_pairs={{0,192},{8,56},{16,208},{24,8},{32,224},{40,24},{48,240},{56,40},{... | collective-permute-start | bytes 12296 | tf_op jit(solution)/shard_map/ppermute | solution.py:50
  134.8 8.5 %collective-permute-start.21 = (f32[8,128]{1,0:T(8,128)S(1)}, f32[8,128]{1,0:T(8,128)S(1)}, u32[]{:S(2)}, u32[]{:S(2)}) collective-permute-start(f32[8,128]{1,0:T(8,128)S(1)} %add.21), channel_id=1, source_target_pairs={{0,128},{8,40},{16,144},{24,56},{32,160},{40,8},{48,176},{56,24},{... | collective-permute-start | bytes 12296 | tf_op jit(solution)/shard_map/ppermute | solution.py:50
  145.2 8.3 %collective-permute-start.22 = (f32[3,192,384]{2,1,0:T(8,128)S(1)}, f32[3,192,384]{2,1,0:T(8,128)S(1)}, u32[]{:S(2)}, u32[]{:S(2)}) collective-permute-start(f32[3,192,384]{2,1,0:T(8,128)S(1)} %shard_map.86), channel_id=1, source_target_pairs={{0,8},{8,0},{1,9},{9,1},{2,10},{10,2},{3,11},{11,3},{4,12},{12,4},... | collective-permute-start | bytes 2654216 | tf_op jit(solution)/shard_map/ppermute | solution.py:38
  (8 other events, 9.2 us)
Sparse Core Ops, SparseCore 0:
  10.4 76.3 all-gather.4
  89.1 35.5 all-gather.6
